TPU v7x, 128 devices: a whole 4x4x4 slice. The times are simulated.
128 devices in a mesh: dp: 8 (over z, y_lo), fsdp: 16 (over y_hi, x, core).
Axes of the slice: x: 4, y: 4 (y_hi: 2, y_lo: 2; y = y_hi * 2 + y_lo), z: 4, core: 2. Of those that a mesh axis runs over, the one named last changes fastest.
Arguments:
- hidden: bfloat16 [2048, 32, 5120], P(('dp', 'fsdp')), may hold values from -6 to 6
- queries: bfloat16 [2048, 32, 2560], P(('dp', 'fsdp')), may hold values from -6 to 6
- out_grad: bfloat16 [2048, 32, 2560], P(('dp', 'fsdp')), may hold values from -6 to 6
- counts: int32 [2048], P(('dp', 'fsdp')), may hold values from 1 to 2
- send_peer: int32 [2048], P(('dp', 'fsdp')), may hold values from 0 to 7, as said below
- recv_from: int32 [2048], P(('dp', 'fsdp')), may hold values from 0 to 7, as said below
- key_weight: bfloat16 [5120, 512], P('fsdp'), may hold values from -0.6 to 0.6
- value_weight: bfloat16 [5120, 512], P('fsdp'), may hold values from -0.078125 to 0.078125
Outputs:
- hidden_grad: bfloat16 [2048, 32, 5120], P(('dp', 'fsdp'))
- key_grad: float32 [5120, 512], P('fsdp')
- value_grad: float32 [5120, 512], P('fsdp')
Inputs may be any that keep to these rules, and one draw needn't show every extreme that they name: Within each fsdp index, every device sends 8 - 1 trajectories, one to each other dp index, and receives one from each; a slot whose send_peer is its own dp index is kept, and an arriving trajectory fills a slot whose recv_from names its sender. recv_from is the inverse of send_peer in the sense above: slot s of device (a, b) with recv_from = c != a receives the unique slot of device (c, b) whose send_peer is a.
All inputs are finite; a program needn't handle non-finite values.
Results may differ from a plain program's by a relative error of at most 0.025.
Values may be sent and summed in bfloat16 or wider, within the bound.
A program may use at most 192 MiB of HBM per device.

v0:
```python
import jax
import jax.numpy as jnp
from jax import lax
from jax.experimental import pallas as pl
from jax.experimental.pallas import tpu as pltpu
from jax.sharding import PartitionSpec as P

HD = 128
JBLK = 16
WIDE = 384
MESH = pl.DeviceIdType.MESH


def place():
    d, f = lax.axis_index("dp"), lax.axis_index("fsdp")
    return lax.rem(lax.div(f, 2), 4), lax.div(f, 8), lax.rem(d, 2), lax.div(d, 2), lax.rem(f, 2)


def device(x, h, l, z, c):
    return (z * 2 + l, (h * 4 + x) * 2 + c)


def gather_kernel(hidden, kw, vw, pair_out, w_out, w, hid, send_sem, recv_sem, local_sem):
    x, h, l, z, c = place()
    rows, width = kw.shape
    cols = 2 * width
    quarter = rows // 4

    def wrap(v):
        return lax.rem(v + 4, 4)

    xp, xm = device(wrap(x + 1), h, l, z, c), device(wrap(x - 1), h, l, z, c)
    zp, zm = device(x, h, l, wrap(z + 1), c), device(x, h, l, wrap(z - 1), c)
    yo, peer = device(x, 1 - h, 1 - l, z, c), device(x, h, l, z, 1 - c)

    hid_copy = pltpu.make_async_copy(hidden, hid, local_sem.at[0])
    hid_copy.start()
    own = (h * 4 + x) * 2 + c
    w[own, :, pl.ds(0, width)] = kw[...]
    w[own, :, pl.ds(width, width)] = vw[...]

    barrier = pltpu.get_barrier_semaphore()
    for other in (xp, xm, zp, zm, yo, peer):
        pl.semaphore_signal(barrier, inc=1, device_id=other, device_id_type=MESH)
    pl.semaphore_wait(barrier, 6)

    number = {}
    started = []

    def copy(name, f, row, col, target):
        i = number.setdefault(name, len(number))
        ref = w.at[f, pl.ds(*row), pl.ds(*col)]
        return pltpu.make_async_remote_copy(
            src_ref=ref, dst_ref=ref, send_sem=send_sem.at[i], recv_sem=recv_sem.at[i],
            device_id=target, device_id_type=MESH,
        )

    def send(name, f, row, col, target):
        one = copy(name, f, row, col, target)
        one.start()
        started.append(one)

    def arrive(name, f, row, col):
        copy(name, f, row, col, peer).wait_recv()

    def block(hh, dx, core=c):
        return (hh * 4 + wrap(x + dx)) * 2 + core

    def part(dz):
        return (pl.multiple_of(wrap(z + dz) * quarter, quarter), quarter)

    def halves(odd):
        first = 256 if odd else 384
        return (WIDE, first), (WIDE + first, cols - WIDE - first)

    side = (h, 1 - h)
    narrow, wide = (WIDE, cols - WIDE), (0, WIDE)
    whole, low, high = (0, rows), (0, rows // 2), (rows // 2, rows // 2)

    send("cy", own, part(0), narrow, yo)
    send("cxp0", own, part(0), narrow, xp)
    send("cxm0", own, part(0), narrow, xm)
    send("own", own, whole, (0, cols), peer)

    def along_z(b, f):
        send(f"zp{b}", f, part(0), narrow, zp)
        send(f"zm{b}", f, part(0), narrow, zm)

    order = [(1, 0), (0, -1), (0, 1), (1, -1), (1, 1), (0, 2), (1, 2)]
    arrive("cy", block(side[1], 0), part(0), narrow)
    send("cxp1", block(side[1], 0), part(0), narrow, xp)
    send("cxm1", block(side[1], 0), part(0), narrow, xm)
    along_z(0, block(side[1], 0))
    for s in (0, 1):
        one, two = halves(s)
        arrive(f"cxp{s}", block(side[s], -1), part(0), narrow)
        send(f"cfp{s}", block(side[s], -1), part(0), one, xp)
        along_z(1 + 2 * s, block(side[s], -1))
        arrive(f"cxm{s}", block(side[s], 1), part(0), narrow)
        send(f"cfm{s}", block(side[s], 1), part(0), two, xm)
        along_z(2 + 2 * s, block(side[s], 1))
    send("ay", own, whole, wide, yo)
    send("axp0", own, whole, wide, xp)
    send("axm0", own, whole, wide, xm)
    for s in (0, 1):
        one, two = halves(s)
        arrive(f"cfp{s}", block(side[s], 2), part(0), one)
        arrive(f"cfm{s}", block(side[s], 2), part(0), two)
        along_z(5 + s, block(side[s], 2))

    def forward_z(b):
        s, dx = order[b]
        one, two = halves(b % 2)
        f = block(side[s], dx)
        arrive(f"zp{b}", f, part(-1), narrow)
        send(f"zfp{b}", f, part(-1), one, zp)
        arrive(f"zm{b}", f, part(1), narrow)
        send(f"zfm{b}", f, part(1), two, zm)

    def finish_z(b):
        s, dx = order[b]
        one, two = halves(b % 2)
        f = block(side[s], dx)
        arrive(f"zfp{b}", f, part(2), one)
        arrive(f"zfm{b}", f, part(2), two)
        send(f"pc{b}", f, whole, narrow, peer)

    def forward_x(s):
        arrive(f"axp{s}", block(side[s], -1), whole, wide)
        send(f"afp{s}", block(side[s], -1), low, wide, xp)
        arrive(f"axm{s}", block(side[s], 1), whole, wide)
        send(f"afm{s}", block(side[s], 1), high, wide, xm)
        send(f"pa{1 + 2 * s}", block(side[s], -1), whole, wide, peer)
        send(f"pa{2 + 2 * s}", block(side[s], 1), whole, wide, peer)

    forward_z(0)
    forward_z(1)
    arrive("ay", block(side[1], 0), whole, wide)
    send("axp1", block(side[1], 0), whole, wide, xp)
    send("axm1", block(side[1], 0), whole, wide, xm)
    send("pa0", block(side[1], 0), whole, wide, peer)
    forward_z(2)
    forward_z(3)
    forward_x(0)
    forward_z(4)
    forward_z(5)
    finish_z(0)
    finish_z(1)
    forward_z(6)
    forward_x(1)
    for b in range(2, 6):
        finish_z(b)
    for s in (0, 1):
        arrive(f"afp{s}", block(side[s], 2), low, wide)
        arrive(f"afm{s}", block(side[s], 2), high, wide)
        send(f"pa{5 + s}", block(side[s], 2), whole, wide, peer)
    finish_z(6)
    arrive("own", block(side[0], 0, 1 - c), whole, (0, cols))
    for b in range(7):
        s, dx = order[b]
        arrive(f"pa{b}", block(side[s], dx, 1 - c), whole, wide)
        arrive(f"pc{b}", block(side[s], dx, 1 - c), whole, narrow)
    w_copy = pltpu.make_async_copy(w, w_out, local_sem.at[1])
    w_copy.start()
    hid_copy.wait()

    blocks = w.shape[0]
    tokens = hidden.shape[0] * hidden.shape[1]
    group = 4

    @pl.loop(0, cols // 256)
    def _(n):
        at = pl.ds(pl.multiple_of(n * 256, 256), 256)
        total = jnp.zeros((tokens, 256), jnp.float32)
        for k in range(blocks // group):
            left = hid[:, :, pl.ds(k * group * rows, group * rows)].reshape(tokens, group * rows)
            right = w[pl.ds(k * group, group), :, at].reshape(group * rows, 256)
            total = total + jnp.dot(left, right, preferred_element_type=jnp.float32)
        pair_out[:, at] = total.astype(jnp.bfloat16)

    w_copy.wait()
    for one in started:
        one.wait_send()


def gather_project(hidden, key_weight, value_weight):
    rows, width = key_weight.shape
    tokens = hidden.shape[0] * hidden.shape[1]
    blocks = lax.axis_size("fsdp")
    vmem = pl.BlockSpec(memory_space=pltpu.VMEM)
    hbm = pl.BlockSpec(memory_space=pl.ANY)
    return pl.pallas_call(
        gather_kernel,
        name="gather_project",
        out_shape=(
            jax.ShapeDtypeStruct((tokens, 2 * width), jnp.bfloat16),
            jax.ShapeDtypeStruct((blocks, rows, 2 * width), jnp.bfloat16),
        ),
        in_specs=[hbm, vmem, vmem],
        out_specs=(vmem, hbm),
        scratch_shapes=[
            pltpu.VMEM((blocks, rows, 2 * width), jnp.bfloat16),
            pltpu.VMEM(hidden.shape, jnp.bfloat16),
            pltpu.SemaphoreType.DMA((64,)),
            pltpu.SemaphoreType.DMA((64,)),
            pltpu.SemaphoreType.DMA((2,)),
        ],
        compiler_params=pltpu.CompilerParams(
            collective_id=0, has_side_effects=True, vmem_limit_bytes=48 << 20
        ),
        cost_estimate=pl.CostEstimate(
            flops=2 * tokens * blocks * rows * 2 * width, bytes_accessed=22 << 20, transcendentals=0
        ),
    )(hidden, key_weight, value_weight)


def attend(counts, queries, grads, pair, delta, group):
    f32, bf16 = jnp.float32, jnp.bfloat16
    tokens = queries.shape[1]
    n = 4 * tokens
    half = pair.shape[1] // 2
    heads = half // HD
    share = queries.shape[2] // half
    scale = HD ** (-0.5)
    at = pl.ds(pl.multiple_of(group * n, n), n)
    slots = pl.ds(group * 4, 4)
    count = [counts[group * 4 + j].astype(f32) for j in range(4)]

    def per_slot(slot):
        return jnp.where(
            slot == 0, count[0], jnp.where(slot == 1, count[1], jnp.where(slot == 2, count[2], count[3]))
        )

    row = lax.broadcasted_iota(jnp.int32, (n, HD), 0)
    own = per_slot(lax.div(row, tokens))
    weight = jnp.where(lax.rem(row, tokens).astype(f32) < own * JBLK, 1.0, 0.0) / own
    lane = lax.broadcasted_iota(jnp.int32, (tokens, share * n), 1)
    slot = lax.div(lax.rem(lane, n), tokens)
    u = lax.broadcasted_iota(jnp.int32, (tokens, share * n), 0)
    allowed = (u <= lax.rem(lane, tokens)) & (u.astype(f32) < per_slot(slot) * JBLK)

    def fold(wide):
        a, b, c, d = (wide[j * tokens : (j + 1) * tokens] for j in range(4))
        return jnp.where(slot == 0, a, jnp.where(slot == 1, b, jnp.where(slot == 2, c, d)))

    def spread(narrow):
        parts = [jnp.where(slot == j, narrow, 0.0) for j in range(4)]
        return jnp.concatenate(parts, axis=0).astype(bf16)

    def across(a, b):
        return lax.dot_general(a, b, (((1,), (1,)), ((), ())), preferred_element_type=f32)

    for g in range(heads):
        cols = [slice((g * share + r) * HD, (g * share + r + 1) * HD) for r in range(share)]
        q = jnp.concatenate([queries[slots, :, c].reshape(n, HD) for c in cols], axis=0)
        od = jnp.concatenate(
            [(grads[slots, :, c].reshape(n, HD).astype(f32) * weight).astype(bf16) for c in cols],
            axis=0,
        )
        key = pair[at, g * HD : (g + 1) * HD]
        value = pair[at, half + g * HD : half + (g + 1) * HD]
        scores = jnp.where(allowed, fold(across(key, q)) * scale, -1e30)
        terms = jnp.exp(scores - jnp.max(scores, axis=0, keepdims=True))
        probs = terms / jnp.sum(terms, axis=0, keepdims=True)
        probs_half = probs.astype(bf16).astype(f32)
        prob_delta = fold(across(value, od))
        row_delta = jnp.sum(probs_half * prob_delta, axis=0, keepdims=True)
        score_delta = probs * (prob_delta - row_delta) * scale
        key_delta = jnp.dot(spread(score_delta), q, preferred_element_type=f32)
        value_delta = jnp.dot(spread(probs_half), od, preferred_element_type=f32)
        delta[at, g * HD : (g + 1) * HD] = key_delta.astype(bf16)
        delta[at, half + g * HD : half + (g + 1) * HD] = value_delta.astype(bf16)


def attend_kernel(counts, queries, grads, pair, delta):
    @pl.loop(0, queries.shape[0] // 4)
    def _(group):
        attend(counts, queries, grads, pair, delta, group)


def attend_all(counts, queries, grads, pair):
    vmem = pl.BlockSpec(memory_space=pltpu.VMEM)
    return pl.pallas_call(
        attend_kernel,
        name="attend",
        out_shape=jax.ShapeDtypeStruct(pair.shape, pair.dtype),
        in_specs=[pl.BlockSpec(memory_space=pltpu.SMEM), vmem, vmem, vmem],
        out_specs=vmem,
        compiler_params=pltpu.CompilerParams(vmem_limit_bytes=48 << 20),
    )(counts, queries, grads, pair)


def reduce_kernel(
    recv, pair, leaving, hidden, w_in, hg_out, gt_out,
    hid, w, dt, arrived, settled, hgb, summed, give, take,
    p0_half, p0_last, p1_half, p1_last, p2_half, p2_last,
    p0_two, p1_two, p2_two, p0_three, p1_three, p2_three, done,
    send_sem, recv_sem, local_sem,
):
    x, h, l, z, c = place()
    me = lax.axis_index("dp")
    y = 2 * h + l
    half = dt.shape[1]
    span = summed.shape[2]
    slots, tokens, _ = hidden.shape
    total = slots * tokens
    f32, bf16 = jnp.float32, jnp.bfloat16

    def wrap(v):
        return lax.rem(v + 4, 4)

    def at(dx=0, dy=0, dz=0, core=c):
        q = wrap(y + dy)
        return device(wrap(x + dx), lax.div(q, 2), lax.rem(q, 2), wrap(z + dz), core)

    xp, xm, x2 = at(dx=1), at(dx=-1), at(dx=2)
    yp, ym, y2 = at(dy=1), at(dy=-1), at(dy=2)
    zp, zm, z2 = at(dz=1), at(dz=-1), at(dz=2)
    peer = at(core=1 - c)
    twin = device(x, h, 1 - l, z, c)
    group = lax.axis_size("dp")
    f = lax.axis_index("fsdp")

    hid_copy = pltpu.make_async_copy(hidden, hid, local_sem.at[0])
    hid_copy.start()
    w_copy = pltpu.make_async_copy(w_in, w, local_sem.at[1])
    w_copy.start()

    others = [(lax.rem(me + j, group), f) for j in range(1, group)]
    others += [xp, xm, x2, device(x, 1 - h, 1 - l, z, c), y2, peer]
    barrier = pltpu.get_barrier_semaphore()
    for other in others:
        pl.semaphore_signal(barrier, inc=1, device_id=other, device_id_type=MESH)
    pl.semaphore_wait(barrier, len(others))

    number = {}
    started = []

    def copy(name, src, dst, target):
        i = number.setdefault(name, len(number))
        return pltpu.make_async_remote_copy(
            src_ref=src, dst_ref=dst, send_sem=send_sem.at[i], recv_sem=recv_sem.at[i],
            device_id=target, device_id_type=MESH,
        )

    def send(name, src, dst, target):
        one = copy(name, src, dst, target)
        one.start()
        started.append(one)

    def arrive(name, dst):
        copy(name, dst, dst, peer).wait_recv()

    def add(*refs):
        value = refs[0][...].astype(f32)
        for ref in refs[1:]:
            value = value + ref[...].astype(f32)
        return value.astype(bf16)

    arrived[me] = jnp.zeros(arrived.shape[1:], bf16)
    for j in range(1, group):
        to = lax.rem(me + j, group)
        send(f"a{j}", leaving.at[to], arrived.at[me], (to, f))
    for t in (0, 1):
        dt[t] = pair[:, t * half : (t + 1) * half].T

    lanes = (pl.ds(0, 256), pl.ds(256, 256), pl.ds(512, 128))
    order = [(0, 2), (1, 2), (1, 1), (0, -1), (0, 1), (1, -1), (0, 0), (1, 0)]

    def index(hh, dx):
        return hh * 4 + wrap(x + dx)

    def term(t, k):
        cols = pl.ds(pl.multiple_of(k * span, 128), span)
        return jnp.dot(dt[t], hid[:, :, cols].reshape(total, span), preferred_element_type=f32)

    def other_half(i):
        k = index(*order[i])
        give[k] = term(1 - c, k).astype(bf16)
        send(f"d{i}", give.at[k], take.at[k], peer)

    def own_half(i):
        k = index(*order[i])
        value = term(c, k)
        arrive(f"d{i}", take.at[k])
        summed[k] = (value + take[k].astype(f32)).astype(bf16)

    def zrows(dz):
        return pl.ds(pl.multiple_of(wrap(z + dz) * 128, 128), 128)

    def part1_first(i):
        k = index(*order[i])
        up, down = (2, -1) if i % 2 == 0 else (1, 2)
        one, two = ("h", "n") if i % 2 == 0 else ("n", "h")
        far_dst, near_dst = p1_half.at[i], p1_last.at[1 if i % 2 == 0 else 0, i]
        dst = {"h": far_dst, "n": near_dst}
        send(f"z{one}{i}", summed.at[k, zrows(up), lanes[1]], dst[one], zp)
        send(f"z{two}{i}", summed.at[k, zrows(down), lanes[1]], dst[two], zm)

    def part1_second(i):
        k = index(*order[i])
        near, target = (1, zp) if i % 2 == 0 else (-1, zm)
        arrive(f"zh{i}", p1_half.at[i])
        ref = summed.at[k, zrows(near), lanes[1]]
        ref[...] = add(ref, p1_half.at[i])
        send(f"zl{i}", ref, p1_last.at[0 if i % 2 == 0 else 1, i], target)

    def part1_last(i):
        k = index(*order[i])
        arrive(f"zn{i}", p1_last.at[1 if i % 2 == 0 else 0, i])
        arrive(f"zl{i}", p1_last.at[0 if i % 2 == 0 else 1, i])
        ref = summed.at[k, zrows(0), lanes[1]]
        ref[...] = add(ref, p1_last.at[0, i], p1_last.at[1, i])

    def yref(dy, dx):
        q = wrap(y + dy)
        rows = pl.ds(pl.multiple_of(lax.rem(q, 2) * 256, 256), 256)
        return summed.at[lax.div(q, 2) * 4 + wrap(x + dx), rows, lanes[2]]

    shifts = (2, 1, -1, 0)

    def part2_first(j):
        dx = shifts[j]
        if j % 2 == 0:
            send(f"yh{j}", yref(2, dx), p2_half.at[j], yp)
            send(f"yn{j}", yref(-1, dx), p2_last.at[1, j], ym)
        else:
            send(f"yn{j}", yref(1, dx), p2_last.at[0, j], yp)
            send(f"yh{j}", yref(2, dx), p2_half.at[j], ym)

    def part2_second(j):
        near, target = (1, yp) if j % 2 == 0 else (-1, ym)
        arrive(f"yh{j}", p2_half.at[j])
        ref = yref(near, shifts[j])
        ref[...] = add(ref, p2_half.at[j])
        send(f"yl{j}", ref, p2_last.at[0 if j % 2 == 0 else 1, j], target)

    def part2_last(j):
        arrive(f"yn{j}", p2_last.at[1 if j % 2 == 0 else 0, j])
        arrive(f"yl{j}", p2_last.at[0 if j % 2 == 0 else 1, j])
        ref = yref(0, shifts[j])
        ref[...] = add(ref, p2_last.at[0, j], p2_last.at[1, j])

    def xref(hh, dx):
        return summed.at[index(hh, dx), :, lanes[0]]

    hid_copy.wait()
    other_half(0)
    other_half(1)
    for i in range(8):
        own_half(i)
        if i == 0:
            send("xh0", xref(0, 2), p0_half.at[0], xp)
        elif i == 1:
            send("xh1", xref(1, 2), p0_half.at[1], xm)
        elif i == 2:
            send("xn1", xref(1, 1), p0_last.at[0, 1], xp)
        elif i == 3:
            send("xn0", xref(0, -1), p0_last.at[1, 0], xm)
        part1_first(i)
        if i == 1:
            part2_first(0)
        elif i == 5:
            part2_first(1)
            part2_first(2)
        elif i == 7:
            part2_first(3)
        if i + 2 < 8:
            other_half(i + 2)
        if i >= 3:
            part1_second(i - 3)
        if i == 5:
            part2_second(0)
    arrive("xh0", p0_half.at[0])
    xref(0, 1)[...] = add(xref(0, 1), p0_half.at[0])
    send("xl0", xref(0, 1), p0_last.at[0, 0], xp)
    arrive("xh1", p0_half.at[1])
    xref(1, -1)[...] = add(xref(1, -1), p0_half.at[1])
    send("xl1", xref(1, -1), p0_last.at[1, 1], xm)
    part1_second(5)
    part2_second(1)
    part2_second(2)

    for j in range(1, group):
        arrive(f"a{j}", arrived.at[lax.rem(me + group - j, group)])
    for s in range(slots):
        source = recv[s]
        kept = pair[pl.ds(s * tokens, tokens), :]
        settled[pl.ds(s * tokens, tokens), :] = jnp.where(source == me, kept, arrived[source])
    w_copy.wait()
    hg_copies = []

    def back(j):
        block = w[2 * j : 2 * j + 2].reshape(span, w.shape[2])
        value = lax.dot_general(
            settled[...], block, (((1,), (1,)), ((), ())), preferred_element_type=f32
        )
        cols = pl.ds(j * span, span)
        hgb[:, :, cols] = value.astype(bf16).reshape(slots, tokens, span)
        one = pltpu.make_async_copy(hgb.at[:, :, cols], hg_out.at[:, :, cols], local_sem.at[2 + j])
        one.start()
        hg_copies.append(one)

    back(0)
    part1_second(6)
    back(1)
    part2_second(3)
    part1_second(7)
    for i in range(4):
        part1_last(i)
    back(2)
    part2_last(0)
    part1_last(4)
    part1_last(5)
    back(3)
    part2_last(1)
    part2_last(2)
    back(4)
    part2_last(3)
    part1_last(6)
    part1_last(7)

    steps = ((1, xp), (-1, xm), (2, x2))
    for n, (dx, target) in enumerate(steps):
        for hh in (0, 1):
            src = summed.at[index(hh, dx), zrows(0), lanes[1]]
            send(f"s1{n}{hh}", src, p1_two.at[n, hh], target)

    def zpiece(dz):
        rows = pl.ds(pl.multiple_of(l * 256 + wrap(z + dz) * 64, 64), 64)
        return summed.at[pl.ds(pl.multiple_of(h * 4, 4), 4), rows, lanes[2]]

    for n, (dz, target) in enumerate(((1, zp), (-1, zm), (2, z2))):
        send(f"s2{n}", zpiece(dz), p2_two.at[n], target)
    for hh in (0, 1):
        arrive(f"xn{hh}", p0_last.at[1 - hh, hh])
        arrive(f"xl{hh}", p0_last.at[hh, hh])
        xref(hh, 0)[...] = add(xref(hh, 0), p0_last.at[0, hh], p0_last.at[1, hh])

    def ypiece(dy):
        q = wrap(y + dy)
        rows = pl.ds(pl.multiple_of(lax.rem(q, 2) * 256, 256), 256)
        return summed.at[lax.div(q, 2) * 4 + x, rows, lanes[0]]

    for n, (dy, target) in enumerate(((1, yp), (-1, ym), (2, y2))):
        send(f"s0{n}", ypiece(dy), p0_two.at[n], target)
    back(5)
    for n in range(3):
        arrive(f"s2{n}", p2_two.at[n])
    zpiece(0)[...] = add(zpiece(0), p2_two.at[0], p2_two.at[1], p2_two.at[2])

    piece_rows = pl.ds(pl.multiple_of(l * 256 + z * 64, 64), 64)
    for n, (dx, target) in enumerate(steps):
        send(f"t2{n}", summed.at[index(h, dx), piece_rows, lanes[2]], p2_three.at[n], target)
    back(6)
    for n in range(3):
        for hh in (0, 1):
            arrive(f"s1{n}{hh}", p1_two.at[n, hh])
    for hh in (0, 1):
        ref = summed.at[index(hh, 0), zrows(0), lanes[1]]
        ref[...] = add(ref, p1_two.at[0, hh], p1_two.at[1, hh], p1_two.at[2, hh])

    def third1(dy):
        q = wrap(y + dy)
        rows = pl.ds(pl.multiple_of(z * 128 + lax.rem(q, 2) * 64, 64), 64)
        return summed.at[lax.div(q, 2) * 4 + x, rows, lanes[1]]

    for n, (dy, target) in enumerate(((1, yp), (-1, ym), (2, y2))):
        send(f"t1{n}", third1(dy), p1_three.at[n], target)
    back(7)
    for n in range(3):
        arrive(f"s0{n}", p0_two.at[n])
    ypiece(0)[...] = add(ypiece(0), p0_two.at[0], p0_two.at[1], p0_two.at[2])

    def third0(dz):
        rows = pl.ds(pl.multiple_of(l * 256 + wrap(z + dz) * 64, 64), 64)
        return summed.at[h * 4 + x, rows, lanes[0]]

    for n, (dz, target) in enumerate(((1, zp), (-1, zm), (2, z2))):
        send(f"t0{n}", third0(dz), p0_three.at[n], target)

    def finish(part, ref, buffer):
        for n in range(3):
            arrive(f"t{part}{n}", buffer.at[n])
        value = add(ref, buffer.at[0], buffer.at[1], buffer.at[2])
        mine = done.at[c, l, z, :, lanes[part]]
        mine[...] = value
        send(f"gy{part}", mine, mine, twin)
        send(f"gp{part}", mine, mine, zp)
        send(f"gm{part}", mine, mine, zm)
        send(f"g2{part}", mine, mine, z2)

    def pass_on(part):
        def piece(ll, dz):
            return done.at[c, ll, wrap(z + dz), :, lanes[part]]

        arrive(f"gy{part}", piece(1 - l, 0))
        send(f"fp{part}", piece(1 - l, 0), piece(1 - l, 0), zp)
        send(f"fm{part}", piece(1 - l, 0), piece(1 - l, 0), zm)
        arrive(f"g2{part}", piece(l, 2))
        send(f"fy{part}", piece(l, 2), piece(l, 2), twin)

    def collect(part):
        def piece(ll, dz):
            return done.at[c, ll, wrap(z + dz), :, lanes[part]]

        arrive(f"gp{part}", piece(l, -1))
        arrive(f"gm{part}", piece(l, 1))
        arrive(f"fp{part}", piece(1 - l, -1))
        arrive(f"fm{part}", piece(1 - l, 1))
        arrive(f"fy{part}", piece(1 - l, 2))
        ref = done.at[c, :, :, :, lanes[part]]
        send(f"e{part}", ref, ref, peer)

    finish(2, summed.at[h * 4 + x, piece_rows, lanes[2]], p2_three)
    finish(1, third1(0), p1_three)
    pass_on(2)
    finish(0, third0(0), p0_three)
    pass_on(1)
    collect(2)
    pass_on(0)
    collect(1)
    collect(0)
    for part in (2, 1, 0):
        arrive(f"e{part}", done.at[1 - c, :, :, :, lanes[part]])
    out_copy = pltpu.make_async_copy(done, gt_out, local_sem.at[10])
    out_copy.start()
    for one in started:
        one.wait_send()
    for one in hg_copies:
        one.wait()
    out_copy.wait()


def reduce_back(recv_from, pair, leaving, hidden, w_blocks):
    blocks, rows, cols = w_blocks.shape
    half, span = cols // 2, 2 * rows
    chips = blocks // 2
    total = pair.shape[0]
    bf16 = jnp.bfloat16
    vmem = pl.BlockSpec(memory_space=pltpu.VMEM)
    hbm = pl.BlockSpec(memory_space=pl.ANY)
    buffer = lambda *shape: pltpu.VMEM(shape, bf16)
    return pl.pallas_call(
        reduce_kernel,
        name="reduce_back",
        out_shape=(
            jax.ShapeDtypeStruct(hidden.shape, bf16),
            jax.ShapeDtypeStruct((2, 2, 4, half // 8, span), bf16),
        ),
        in_specs=[pl.BlockSpec(memory_space=pltpu.SMEM), vmem, vmem, hbm, hbm],
        out_specs=(hbm, hbm),
        scratch_shapes=[
            buffer(*hidden.shape),
            buffer(blocks, rows, cols),
            buffer(2, half, total),
            buffer(*leaving.shape),
            buffer(total, cols),
            buffer(*hidden.shape),
            buffer(chips, half, span),
            buffer(chips, half, span),
            buffer(chips, half, span),
            buffer(2, half, 256),
            buffer(2, 2, half, 256),
            buffer(8, half // 4, 256),
            buffer(2, 8, half // 4, 256),
            buffer(4, half // 2, 128),
            buffer(2, 4, half // 2, 128),
            buffer(3, half // 2, 256),
            buffer(3, 2, half // 4, 256),
            buffer(3, 4, half // 8, 128),
            buffer(3, half // 8, 256),
            buffer(3, half // 8, 256),
            buffer(3, half // 8, 128),
            buffer(2, 2, 4, half // 8, span),
            pltpu.SemaphoreType.DMA((112,)),
            pltpu.SemaphoreType.DMA((112,)),
            pltpu.SemaphoreType.DMA((11,)),
        ],
        compiler_params=pltpu.CompilerParams(
            collective_id=1, has_side_effects=True, vmem_limit_bytes=60 << 20
        ),
        cost_estimate=pl.CostEstimate(
            flops=4 * total * blocks * rows * cols, bytes_accessed=22 << 20, transcendentals=0
        ),
    )(recv_from, pair, leaving, hidden, w_blocks)


def finish_kernel(hg_in, pieces_in, hg_out, key_grad, value_grad, hg, pieces, sem):
    chunks = 8
    step = hg.shape[0] // chunks
    first = pltpu.make_async_copy(pieces_in, pieces, sem.at[2 * chunks])
    first.start()

    def chunk(i, src, dst, offset):
        at = pl.ds(i * step, step)
        return pltpu.make_async_copy(src.at[at], dst.at[at], sem.at[offset + i])

    for i in range(chunks):
        chunk(i, hg_in, hg, 0).start()
    first.wait()
    for i in range(chunks):
        chunk(i, hg_in, hg, 0).wait()
        chunk(i, hg, hg_out, chunks).start()
    core = lax.rem(lax.axis_index("fsdp"), 2)
    rows, width = key_grad.shape
    for t, out in enumerate((key_grad, value_grad)):
        outer = pieces[t].reshape(width, 2 * rows)
        inner = jnp.concatenate(
            [pieces[t, l, z, :, 256:512] for z in range(4) for l in range(2)], axis=0
        )
        grads = jnp.concatenate([outer[:, :256], inner, outer[:, 512:]], axis=1)
        grads = grads.astype(jnp.float32)
        out[...] = jnp.where(core == 0, grads[:, :rows], grads[:, rows:]).T
    for i in range(chunks):
        chunk(i, hg, hg_out, chunks).wait()


def finish(hidden_grad, pieces):
    rows, width = pieces.shape[-1] // 2, pieces.shape[1] * pieces.shape[2] * pieces.shape[3]
    vmem = pl.BlockSpec(memory_space=pltpu.VMEM)
    hbm = pl.BlockSpec(memory_space=pl.ANY)
    grad = jax.ShapeDtypeStruct((rows, width), jnp.float32)
    return pl.pallas_call(
        finish_kernel,
        name="finish",
        out_shape=(jax.ShapeDtypeStruct(hidden_grad.shape, hidden_grad.dtype), grad, grad),
        in_specs=[hbm, hbm],
        out_specs=(hbm, vmem, vmem),
        scratch_shapes=[
            pltpu.VMEM(hidden_grad.shape, hidden_grad.dtype),
            pltpu.VMEM(pieces.shape, pieces.dtype),
            pltpu.SemaphoreType.DMA((17,)),
        ],
        compiler_params=pltpu.CompilerParams(vmem_limit_bytes=60 << 20),
    )(hidden_grad, pieces)


def block_plan(send_peer, recv_from, own_group, group_count):
    peer_ids = jnp.arange(group_count, dtype=jnp.int32)
    staying = recv_from == own_group
    chosen = ((send_peer[None, :] == peer_ids[:, None]) & (peer_ids[:, None] != own_group)).astype(
        jnp.bfloat16
    )
    placing = (
        (recv_from[:, None] == peer_ids[None, :]) & jnp.logical_not(staying)[:, None]
    ).astype(jnp.bfloat16)
    return (chosen, placing, staying)


def select_rows(chosen, source):
    return jnp.einsum("ps,stf->ptf", chosen, source, preferred_element_type=jnp.float32).astype(
        jnp.bfloat16
    )


def body(hidden, queries, out_grad, counts, send_peer, recv_from, key_weight, value_weight):
    width = key_weight.shape[1]
    pair, w_blocks = gather_project(hidden, key_weight, value_weight)
    group_count = lax.axis_size("dp")
    own_group = lax.axis_index("dp")
    chosen, placing, staying = block_plan(send_peer, recv_from, own_group, group_count)
    pair_delta = attend_all(counts, queries, out_grad, pair)
    slots, tokens = hidden.shape[0], hidden.shape[1]
    pair_rows = pair_delta.reshape(slots, tokens, 2 * width)
    leaving = select_rows(chosen, pair_rows)
    hidden_grad, pieces = reduce_back(recv_from, pair_delta, leaving, hidden, w_blocks)
    return finish(hidden_grad, pieces)


def solution(mesh):
    return jax.shard_map(
        body,
        mesh=mesh,
        in_specs=(
            P(("dp", "fsdp"), None, None),
            P(("dp", "fsdp"), None, None),
            P(("dp", "fsdp"), None, None),
            P(("dp", "fsdp")),
            P(("dp", "fsdp")),
            P(("dp", "fsdp")),
            P("fsdp", None),
            P("fsdp", None),
        ),
        out_specs=(P(("dp", "fsdp"), None, None), P("fsdp", None), P("fsdp", None)),
        check_vma=False,
    )
```

profile of v0, /device:TPU:1, one launch (start us, length us, event | category | flops | bytes accessed | tf_op | source)
XLA Modules:
  0.0 121.1 jit_solution(4580363840261013424)
XLA Ops:
  0.6 0.0 copy-start.3
  0.7 1.0 copy-done.3
  1.6 0.0 copy-start.4
  1.6 1.0 copy-done.4
  2.6 0.0 copy-start.1
  2.6 0.0 copy-start.2
  2.6 46.3 %gather_project.1 = (bf16[512,1024]{1,0:T(8,128)(2,1)S(1)}, bf16[16,320,1024]{2,1,0:T(8,128)(2,1)}) custom-call(bf16[16,32,5120]{2,1,0:T(8,128)(2,1)} %hidden.3, bf16[320,512]{1,0:T(8,128)(2,1)S(1)} %copy-done.3, bf16[320,512]{1,0:T(8,128)(2,1)S(1)} %copy-done.4), custom_call_target="tpu_custom_call" | custom-call | flops 5368709120 | bytes 23068672 | tf_op jit(solution)/shard_map/gather_project/pallas_call | solution.py:192
  48.9 0.0 copy-start.5
  48.9 0.0 copy-done.1
  48.9 0.0 copy-done.2
  48.9 8.0 %attend.1.pair = bf16[512,1024]{1,0:T(8,128)(2,1)S(1)} custom-call(s32[16]{0:T(128)S(1)} %copy-done.2, bf16[16,32,2560]{2,1,0:T(8,128)(2,1)S(1)} %copy-done.1, bf16[16,32,2560]{2,1,0:T(8,128)(2,1)} %grads.1, bf16[512,1024]{1,0:T(8,128)(2,1)S(1)} %get-tuple-element.7.pair), custom_call_target="tpu_custom_call" | custom-call | tf_op jit(solution)/shard_map/attend/pallas_call | solution.py:283
  57.0 0.0 copy-start
  57.0 0.0 copy-done.5
  57.0 0.7 fusion
  57.7 1.1 copy.16.leaving
  58.8 0.0 copy-done
  58.8 56.1 %reduce_back.1 = (bf16[16,32,5120]{2,1,0:T(8,128)(2,1)}, bf16[2,2,4,64,640]{4,3,2,1,0:T(8,128)(2,1)}) custom-call(s32[16]{0:T(128)} %recv.1, bf16[512,1024]{1,0:T(8,128)(2,1)} %copy-done, bf16[8,32,1024]{2,1,0:T(8,128)(2,1)} %copy.16.leaving, bf16[16,32,5120]{2,1,0:T(8,128)(2,1)} %hidden.3, bf16[16,320,1024]{2,1,0:T(8,128)(2,1)} %get-tuple-element.8.w_in), custom_call_target="tpu_custom_call" | custom-call | flops 10737418240 | bytes 23068672 | tf_op jit(solution)/shard_map/reduce_back/pallas_call | solution.py:644
  114.9 6.0 %finish.1 = (bf16[16,32,5120]{2,1,0:T(8,128)(2,1)}, f32[320,512]{1,0:T(8,128)}, f32[320,512]{1,0:T(8,128)}) custom-call(bf16[16,32,5120]{2,1,0:T(8,128)(2,1)} %get-tuple-element.9.hg_in, bf16[2,2,4,64,640]{4,3,2,1,0:T(8,128)(2,1)} %get-tuple-element.10.pieces_in), custom_call_target="tpu_custom_call" | custom-call | tf_op jit(solution)/shard_map/finish/pallas_call | solution.py:724
  (1 shorter events, 0.0 us)
Async XLA Ops:
  0.6 1.0 copy-start.3
  1.6 1.0 copy-start.4
  2.6 46.3 %copy-start.1 = (bf16[16,32,2560]{2,1,0:T(8,128)(2,1)S(1)}, bf16[16,32,2560]{2,1,0:T(8,128)(2,1)}, u32[]{:S(2)}) copy-start(bf16[16,32,2560]{2,1,0:T(8,128)(2,1)} %queries.1) | copy-start | bytes 7864324
  2.6 46.3 %copy-start.2 = (s32[16]{0:T(128)S(1)}, s32[16]{0:T(128)}, u32[]{:S(2)}) copy-start(s32[16]{0:T(128)} %counts.1) | copy-start | bytes 196
  48.9 8.1 %copy-start.5 = (s32[16]{0:T(128)S(1)}, s32[16]{0:T(128)}, u32[]{:S(2)}) copy-start(s32[16]{0:T(128)} %param.12) | copy-start | bytes 196
  57.0 1.8 %copy-start = (bf16[512,1024]{1,0:T(8,128)(2,1)}, bf16[512,1024]{1,0:T(8,128)(2,1)S(1)}, u32[]{:S(2)}) copy-start(bf16[512,1024]{1,0:T(8,128)(2,1)S(1)} %attend.1.pair) | copy-start | bytes 3145732
where the time goes:
time: 121 us
  Pallas kernels  116 us (96%)
  local copies, waits for them, and re-layouts  3.05 us (3%)
    pallas_call x1, Pallas kernels, reduce_back(): pl.pallas_call(reduce_kernel, name='reduce_back', out_shape=(jax.ShapeDty...  56.1 us
    pallas_call x1, Pallas kernels, gather_project(): pl.pallas_call(gather_kernel, name='gather_project', out_shape=(jax.Shape...  46.3 us
    pallas_call x1, Pallas kernels, attend_all(): pl.pallas_call(attend_kernel, name='attend', out_shape=jax.ShapeDtypeStru...  8.03 us
    pallas_call x1, Pallas kernels, finish(): pl.pallas_call(finish_kernel, name='finish', out_shape=(jax.ShapeDtypeStr...  6.04 us

commit v1 on v0

v1 whole, which is shorter than its diff:
```python
import jax
import jax.numpy as jnp
from jax import lax
from jax.experimental import pallas as pl
from jax.experimental.pallas import tpu as pltpu
from jax.sharding import PartitionSpec as P

HD = 128
JBLK = 16
WIDE = 384
MESH = pl.DeviceIdType.MESH


def place():
    d, f = lax.axis_index("dp"), lax.axis_index("fsdp")
    return lax.rem(lax.div(f, 2), 4), lax.div(f, 8), lax.rem(d, 2), lax.div(d, 2), lax.rem(f, 2)


def device(x, h, l, z, c):
    return (z * 2 + l, (h * 4 + x) * 2 + c)


def attend(counts, queries, grads, pair, delta, group):
    f32, bf16 = jnp.float32, jnp.bfloat16
    tokens = queries.shape[1]
    n = 4 * tokens
    half = pair.shape[1] // 2
    heads = half // HD
    share = queries.shape[2] // half
    scale = HD ** (-0.5)
    at = pl.ds(pl.multiple_of(group * n, n), n)
    slots = pl.ds(group * 4, 4)
    count = [counts[group * 4 + j].astype(f32) for j in range(4)]

    def per_slot(slot):
        return jnp.where(
            slot == 0, count[0], jnp.where(slot == 1, count[1], jnp.where(slot == 2, count[2], count[3]))
        )

    row = lax.broadcasted_iota(jnp.int32, (n, HD), 0)
    own = per_slot(lax.div(row, tokens))
    weight = jnp.where(lax.rem(row, tokens).astype(f32) < own * JBLK, 1.0, 0.0) / own
    lane = lax.broadcasted_iota(jnp.int32, (tokens, share * n), 1)
    slot = lax.div(lax.rem(lane, n), tokens)
    u = lax.broadcasted_iota(jnp.int32, (tokens, share * n), 0)
    allowed = (u <= lax.rem(lane, tokens)) & (u.astype(f32) < per_slot(slot) * JBLK)

    def fold(wide):
        a, b, c, d = (wide[j * tokens : (j + 1) * tokens] for j in range(4))
        return jnp.where(slot == 0, a, jnp.where(slot == 1, b, jnp.where(slot == 2, c, d)))

    def spread(narrow):
        parts = [jnp.where(slot == j, narrow, 0.0) for j in range(4)]
        return jnp.concatenate(parts, axis=0).astype(bf16)

    def across(a, b):
        return lax.dot_general(a, b, (((1,), (1,)), ((), ())), preferred_element_type=f32)

    for g in range(heads):
        cols = [slice((g * share + r) * HD, (g * share + r + 1) * HD) for r in range(share)]
        q = jnp.concatenate([queries[slots, :, c].reshape(n, HD) for c in cols], axis=0)
        od = jnp.concatenate(
            [(grads[slots, :, c].reshape(n, HD).astype(f32) * weight).astype(bf16) for c in cols],
            axis=0,
        )
        key = pair[at, g * HD : (g + 1) * HD]
        value = pair[at, half + g * HD : half + (g + 1) * HD]
        scores = jnp.where(allowed, fold(across(key, q)) * scale, -1e30)
        terms = jnp.exp(scores - jnp.max(scores, axis=0, keepdims=True))
        probs = terms / jnp.sum(terms, axis=0, keepdims=True)
        probs_half = probs.astype(bf16).astype(f32)
        prob_delta = fold(across(value, od))
        row_delta = jnp.sum(probs_half * prob_delta, axis=0, keepdims=True)
        score_delta = probs * (prob_delta - row_delta) * scale
        key_delta = jnp.dot(spread(score_delta), q, preferred_element_type=f32)
        value_delta = jnp.dot(spread(probs_half), od, preferred_element_type=f32)
        delta[at, g * HD : (g + 1) * HD] = key_delta.astype(bf16)
        delta[at, half + g * HD : half + (g + 1) * HD] = value_delta.astype(bf16)


def main_kernel(
    counts, send_peer, recv_from, kw, vw, hidden, queries, out_grad, hg_out, gt_out,
    w, hid, qs, gs, acc, pair, delta, leaving, arrived, settled, dt, summed, give, take,
    p0_half, p0_last, p1_half, p1_last, p2_half, p2_last,
    p0_two, p1_two, p2_two, p0_three, p1_three, p2_three, done,
    send_sem, recv_sem, local_sem,
):
    x, h, l, z, c = place()
    me, f = lax.axis_index("dp"), lax.axis_index("fsdp")
    group = lax.axis_size("dp")
    y = 2 * h + l
    rows, width = kw.shape
    cols = 2 * width
    quarter = rows // 4
    half = width
    span = 2 * rows
    slots, tokens, _ = hidden.shape
    total = slots * tokens
    f32, bf16 = jnp.float32, jnp.bfloat16

    def wrap(v):
        return lax.rem(v + 4, 4)

    def at(dx=0, dy=0, dz=0, core=c):
        q = wrap(y + dy)
        return device(wrap(x + dx), lax.div(q, 2), lax.rem(q, 2), wrap(z + dz), core)

    xp, xm, x2 = at(dx=1), at(dx=-1), at(dx=2)
    yp, ym, y2 = at(dy=1), at(dy=-1), at(dy=2)
    zp, zm, z2 = at(dz=1), at(dz=-1), at(dz=2)
    peer = at(core=1 - c)
    twin, yo = device(x, h, 1 - l, z, c), device(x, 1 - h, 1 - l, z, c)

    loads = []
    for i, (src, dst) in enumerate(((hidden, hid), (queries, qs), (out_grad, gs))):
        loads.append(pltpu.make_async_copy(src, dst, local_sem.at[i]))
        loads[-1].start()
    hid_copy = loads[0]
    own = (h * 4 + x) * 2 + c
    w[own, :, pl.ds(0, width)] = kw[...]
    w[own, :, pl.ds(width, width)] = vw[...]

    others = [(lax.rem(me + j, group), f) for j in range(1, group)]
    others += [xp, xm, x2, yo, y2, peer]
    barrier = pltpu.get_barrier_semaphore()
    for other in others:
        pl.semaphore_signal(barrier, inc=1, device_id=other, device_id_type=MESH)
    pl.semaphore_wait(barrier, len(others))

    number = {}
    started = []

    def copy(name, src, dst, target):
        i = number.setdefault(name, len(number))
        return pltpu.make_async_remote_copy(
            src_ref=src, dst_ref=dst, send_sem=send_sem.at[i], recv_sem=recv_sem.at[i],
            device_id=target, device_id_type=MESH,
        )

    def send(name, src, dst, target):
        one = copy(name, src, dst, target)
        one.start()
        started.append(one)

    def arrive(name, dst):
        copy(name, dst, dst, peer).wait_recv()

    def w_send(name, block, row, col, target):
        ref = w.at[block, pl.ds(*row), pl.ds(*col)]
        send(name, ref, ref, target)

    def w_arrive(name, block, row, col):
        arrive(name, w.at[block, pl.ds(*row), pl.ds(*col)])

    def block(hh, dx, core=c):
        return (hh * 4 + wrap(x + dx)) * 2 + core

    def part(dz):
        return (pl.multiple_of(wrap(z + dz) * quarter, quarter), quarter)

    def halves(odd):
        first = 256 if odd else 384
        return (WIDE, first), (WIDE + first, cols - WIDE - first)

    side = (h, 1 - h)
    narrow, wide = (WIDE, cols - WIDE), (0, WIDE)
    whole, low, high = (0, rows), (0, rows // 2), (rows // 2, rows // 2)

    w_send("cy", own, part(0), narrow, yo)
    w_send("cxp0", own, part(0), narrow, xp)
    w_send("cxm0", own, part(0), narrow, xm)
    w_send("own", own, whole, (0, cols), peer)

    def along_z(b, f):
        w_send(f"zp{b}", f, part(0), narrow, zp)
        w_send(f"zm{b}", f, part(0), narrow, zm)

    blocks_in = [(1, 0), (0, -1), (0, 1), (1, -1), (1, 1), (0, 2), (1, 2)]

    def source(b):
        return block(side[blocks_in[b][0]], blocks_in[b][1])

    w_arrive("cy", source(0), part(0), narrow)
    w_send("cxp1", source(0), part(0), narrow, xp)
    w_send("cxm1", source(0), part(0), narrow, xm)
    along_z(0, source(0))
    for s in (0, 1):
        one, two = halves(s)
        w_arrive(f"cxp{s}", block(side[s], -1), part(0), narrow)
        w_send(f"cfp{s}", block(side[s], -1), part(0), one, xp)
        w_arrive(f"cxm{s}", block(side[s], 1), part(0), narrow)
        w_send(f"cfm{s}", block(side[s], 1), part(0), two, xm)
        if s == 0:
            along_z(1, source(1))
            along_z(2, source(2))
    w_send("ay", own, whole, wide, yo)
    w_send("axp0", own, whole, wide, xp)
    w_send("axm0", own, whole, wide, xm)
    for s in (0, 1):
        one, two = halves(s)
        w_arrive(f"cfp{s}", source(5 + s), part(0), one)
        w_arrive(f"cfm{s}", source(5 + s), part(0), two)

    def forward_z(b):
        s, dx = blocks_in[b]
        one, two = halves(b % 2)
        f = block(side[s], dx)
        w_arrive(f"zp{b}", f, part(-1), narrow)
        w_send(f"zfp{b}", f, part(-1), one, zp)
        w_arrive(f"zm{b}", f, part(1), narrow)
        w_send(f"zfm{b}", f, part(1), two, zm)

    def finish_z(b):
        s, dx = blocks_in[b]
        one, two = halves(b % 2)
        f = block(side[s], dx)
        w_arrive(f"zfp{b}", f, part(2), one)
        w_arrive(f"zfm{b}", f, part(2), two)
        w_send(f"pc{b}", f, whole, narrow, peer)

    def forward_x(s):
        w_arrive(f"axp{s}", block(side[s], -1), whole, wide)
        w_send(f"afp{s}", block(side[s], -1), low, wide, xp)
        w_arrive(f"axm{s}", block(side[s], 1), whole, wide)
        w_send(f"afm{s}", block(side[s], 1), high, wide, xm)
        w_send(f"pa{1 + 2 * s}", block(side[s], -1), whole, wide, peer)
        w_send(f"pa{2 + 2 * s}", block(side[s], 1), whole, wide, peer)

    def finish_x(s):
        w_arrive(f"afp{s}", source(5 + s), low, wide)
        w_arrive(f"afm{s}", source(5 + s), high, wide)
        w_send(f"pa{5 + s}", source(5 + s), whole, wide, peer)

    def project(b):
        if b < 0:
            w_arrive("own", block(h, 0, 1 - c), whole, (0, cols))
            k = h * 4 + x
        else:
            s, dx = blocks_in[b]
            w_arrive(f"pa{b}", block(side[s], dx, 1 - c), whole, wide)
            w_arrive(f"pc{b}", block(side[s], dx, 1 - c), whole, narrow)
            k = side[s] * 4 + wrap(x + dx)
        span = 2 * rows
        left = pl.ds(pl.multiple_of(k * span, 128), span)
        right = pl.ds(pl.multiple_of(k * 2, 2), 2)

        @pl.loop(0, cols // 256)
        def _(n):
            at = pl.ds(pl.multiple_of(n * 256, 256), 256)
            value = jnp.dot(
                hid[:, :, left].reshape(total, span),
                w[right, :, at].reshape(span, 256),
                preferred_element_type=jnp.float32,
            )
            if b < 0:
                acc[:, at] = value
            elif b < 6:
                acc[:, at] += value
            else:
                pair[:, at] = (acc[:, at] + value).astype(jnp.bfloat16)

    forward_z(0)
    along_z(3, source(3))
    forward_z(1)
    along_z(4, source(4))
    w_arrive("ay", source(0), whole, wide)
    w_send("axp1", source(0), whole, wide, xp)
    w_send("axm1", source(0), whole, wide, xm)
    w_send("pa0", source(0), whole, wide, peer)
    hid_copy.wait()
    project(-1)
    forward_z(2)
    along_z(5, source(5))
    forward_z(3)
    along_z(6, source(6))
    forward_x(0)
    finish_z(0)
    forward_z(4)
    finish_z(1)
    project(0)
    forward_z(5)
    forward_x(1)
    finish_z(2)
    project(1)
    forward_z(6)
    finish_z(3)
    project(2)
    finish_z(4)
    project(3)
    finish_x(0)
    finish_z(5)
    project(4)
    finish_x(1)
    finish_z(6)
    project(5)
    project(6)

    loads[1].wait()
    loads[2].wait()

    @pl.loop(0, slots // 4)
    def _(four):
        attend(counts, qs, gs, pair, delta, four)

    def add(*refs):
        value = refs[0][...].astype(f32)
        for ref in refs[1:]:
            value = value + ref[...].astype(f32)
        return value.astype(bf16)

    arrived[me] = jnp.zeros(arrived.shape[1:], bf16)
    for j in range(1, group):
        to = lax.rem(me + j, group)
        chosen = delta[pl.ds(0, tokens), :]
        for s in range(1, slots):
            here = delta[pl.ds(s * tokens, tokens), :]
            chosen = jnp.where(send_peer[s] == to, here, chosen)
        leaving[to] = chosen
        send(f"a{j}", leaving.at[to], arrived.at[me], (to, f))
    for t in (0, 1):
        dt[t] = delta[:, t * half : (t + 1) * half].T

    lanes = (pl.ds(0, 256), pl.ds(256, 384), pl.ds(256, 384))
    rest = (pl.ds(0, 64), pl.ds(0, 32), pl.ds(32, 32))
    order = [(0, 2), (1, 2), (1, 1), (0, -1), (0, 1), (1, -1), (0, 0), (1, 0)]

    def index(hh, dx):
        return hh * 4 + wrap(x + dx)

    def term(t, k):
        cut = pl.ds(pl.multiple_of(k * span, 128), span)
        return jnp.dot(dt[t], hid[:, :, cut].reshape(total, span), preferred_element_type=f32)

    def other_half(i):
        k = index(*order[i])
        give[k] = term(1 - c, k).astype(bf16).reshape(give.shape[1:])
        send(f"d{i}", give.at[k], take.at[k], peer)

    def own_half(i):
        k = index(*order[i])
        value = term(c, k)
        arrive(f"d{i}", take.at[k])
        summed[k] = (value + take[k].reshape(value.shape).astype(f32)).astype(bf16)

    def zrows(dz):
        return pl.ds(pl.multiple_of(wrap(z + dz) * 64, 64), 64)

    def part1_first(i):
        k = index(*order[i])
        up, down = (2, -1) if i % 2 == 0 else (1, 2)
        one, two = ("h", "n") if i % 2 == 0 else ("n", "h")
        far_dst, near_dst = p1_half.at[i], p1_last.at[1 if i % 2 == 0 else 0, i]
        dst = {"h": far_dst, "n": near_dst}
        send(f"z{one}{i}", summed.at[k, zrows(up), lanes[1]], dst[one], zp)
        send(f"z{two}{i}", summed.at[k, zrows(down), lanes[1]], dst[two], zm)

    def part1_second(i):
        k = index(*order[i])
        near, target = (1, zp) if i % 2 == 0 else (-1, zm)
        arrive(f"zh{i}", p1_half.at[i])
        ref = summed.at[k, zrows(near), lanes[1]]
        ref[...] = add(ref, p1_half.at[i])
        send(f"zl{i}", ref, p1_last.at[0 if i % 2 == 0 else 1, i], target)

    def part1_last(i):
        k = index(*order[i])
        arrive(f"zn{i}", p1_last.at[1 if i % 2 == 0 else 0, i])
        arrive(f"zl{i}", p1_last.at[0 if i % 2 == 0 else 1, i])
        ref = summed.at[k, zrows(0), lanes[1]]
        ref[...] = add(ref, p1_last.at[0, i], p1_last.at[1, i])

    def yref(dy, dx):
        q = wrap(y + dy)
        lower = pl.ds(pl.multiple_of(256 + lax.rem(q, 2) * 128, 128), 128)
        return summed.at[lax.div(q, 2) * 4 + wrap(x + dx), lower, lanes[2]]

    shifts = (2, 1, -1, 0)

    def part2_first(j):
        dx = shifts[j]
        if j % 2 == 0:
            send(f"yh{j}", yref(2, dx), p2_half.at[j], yp)
            send(f"yn{j}", yref(-1, dx), p2_last.at[1, j], ym)
        else:
            send(f"yn{j}", yref(1, dx), p2_last.at[0, j], yp)
            send(f"yh{j}", yref(2, dx), p2_half.at[j], ym)

    def part2_second(j):
        near, target = (1, yp) if j % 2 == 0 else (-1, ym)
        arrive(f"yh{j}", p2_half.at[j])
        ref = yref(near, shifts[j])
        ref[...] = add(ref, p2_half.at[j])
        send(f"yl{j}", ref, p2_last.at[0 if j % 2 == 0 else 1, j], target)

    def part2_last(j):
        arrive(f"yn{j}", p2_last.at[1 if j % 2 == 0 else 0, j])
        arrive(f"yl{j}", p2_last.at[0 if j % 2 == 0 else 1, j])
        ref = yref(0, shifts[j])
        ref[...] = add(ref, p2_last.at[0, j], p2_last.at[1, j])

    def xref(hh, dx):
        return summed.at[index(hh, dx), :, lanes[0]]

    other_half(0)
    other_half(1)
    for i in range(8):
        own_half(i)
        if i == 0:
            send("xh0", xref(0, 2), p0_half.at[0], xp)
        elif i == 1:
            send("xh1", xref(1, 2), p0_half.at[1], xm)
        elif i == 2:
            send("xn1", xref(1, 1), p0_last.at[0, 1], xp)
        elif i == 3:
            send("xn0", xref(0, -1), p0_last.at[1, 0], xm)
        part1_first(i)
        if i == 1:
            part2_first(0)
        elif i == 5:
            part2_first(1)
            part2_first(2)
        elif i == 7:
            part2_first(3)
        if i + 2 < 8:
            other_half(i + 2)
        if i >= 3:
            part1_second(i - 3)
        if i == 5:
            part2_second(0)
    arrive("xh0", p0_half.at[0])
    xref(0, 1)[...] = add(xref(0, 1), p0_half.at[0])
    send("xl0", xref(0, 1), p0_last.at[0, 0], xp)
    arrive("xh1", p0_half.at[1])
    xref(1, -1)[...] = add(xref(1, -1), p0_half.at[1])
    send("xl1", xref(1, -1), p0_last.at[1, 1], xm)
    part1_second(5)
    part2_second(1)
    part2_second(2)

    for j in range(1, group):
        arrive(f"a{j}", arrived.at[lax.rem(me + group - j, group)])
    for s in range(slots):
        source = recv_from[s]
        kept = delta[pl.ds(s * tokens, tokens), :]
        settled[pl.ds(s * tokens, tokens), :] = jnp.where(source == me, kept, arrived[source])
    hg_copies = []

    def back(j):
        block = w[2 * j : 2 * j + 2].reshape(span, w.shape[2])
        value = lax.dot_general(
            settled[...], block, (((1,), (1,)), ((), ())), preferred_element_type=f32
        )
        take[j] = value.astype(bf16).reshape(take.shape[1:])
        one = pltpu.make_async_copy(
            take.at[j], hg_out.at[:, :, pl.ds(j * span, span)], local_sem.at[4 + j]
        )
        one.start()
        hg_copies.append(one)

    back(0)
    part1_second(6)
    back(1)
    part2_second(3)
    part1_second(7)
    for i in range(4):
        part1_last(i)
    back(2)
    part2_last(0)
    part1_last(4)
    part1_last(5)
    back(3)
    part2_last(1)
    part2_last(2)
    back(4)
    part2_last(3)
    part1_last(6)
    part1_last(7)

    steps = ((1, xp), (-1, xm), (2, x2))
    for n, (dx, target) in enumerate(steps):
        for hh in (0, 1):
            src = summed.at[index(hh, dx), zrows(0), lanes[1]]
            send(f"s1{n}{hh}", src, p1_two.at[n, hh], target)

    def zpiece(dz):
        lower = pl.ds(pl.multiple_of(256 + l * 128 + wrap(z + dz) * 32, 32), 32)
        return summed.at[pl.ds(pl.multiple_of(h * 4, 4), 4), lower, lanes[2]]

    for n, (dz, target) in enumerate(((1, zp), (-1, zm), (2, z2))):
        send(f"s2{n}", zpiece(dz), p2_two.at[n], target)
    for hh in (0, 1):
        arrive(f"xn{hh}", p0_last.at[1 - hh, hh])
        arrive(f"xl{hh}", p0_last.at[hh, hh])
        xref(hh, 0)[...] = add(xref(hh, 0), p0_last.at[0, hh], p0_last.at[1, hh])

    def ypiece(dy):
        q = wrap(y + dy)
        some = pl.ds(pl.multiple_of(lax.rem(q, 2) * 256, 256), 256)
        return summed.at[lax.div(q, 2) * 4 + x, some, lanes[0]]

    for n, (dy, target) in enumerate(((1, yp), (-1, ym), (2, y2))):
        send(f"s0{n}", ypiece(dy), p0_two.at[n], target)
    back(5)
    for n in range(3):
        arrive(f"s2{n}", p2_two.at[n])
    zpiece(0)[...] = add(zpiece(0), p2_two.at[0], p2_two.at[1], p2_two.at[2])

    piece_rows = pl.ds(pl.multiple_of(256 + l * 128 + z * 32, 32), 32)
    for n, (dx, target) in enumerate(steps):
        send(f"t2{n}", summed.at[index(h, dx), piece_rows, lanes[2]], p2_three.at[n], target)
    back(6)
    for n in range(3):
        for hh in (0, 1):
            arrive(f"s1{n}{hh}", p1_two.at[n, hh])
    for hh in (0, 1):
        ref = summed.at[index(hh, 0), zrows(0), lanes[1]]
        ref[...] = add(ref, p1_two.at[0, hh], p1_two.at[1, hh], p1_two.at[2, hh])

    def third1(dy):
        q = wrap(y + dy)
        some = pl.ds(pl.multiple_of(z * 64 + lax.rem(q, 2) * 32, 32), 32)
        return summed.at[lax.div(q, 2) * 4 + x, some, lanes[1]]

    for n, (dy, target) in enumerate(((1, yp), (-1, ym), (2, y2))):
        send(f"t1{n}", third1(dy), p1_three.at[n], target)
    back(7)
    for n in range(3):
        arrive(f"s0{n}", p0_two.at[n])
    ypiece(0)[...] = add(ypiece(0), p0_two.at[0], p0_two.at[1], p0_two.at[2])

    def third0(dz):
        some = pl.ds(pl.multiple_of(l * 256 + wrap(z + dz) * 64, 64), 64)
        return summed.at[h * 4 + x, some, lanes[0]]

    for n, (dz, target) in enumerate(((1, zp), (-1, zm), (2, z2))):
        send(f"t0{n}", third0(dz), p0_three.at[n], target)

    def finish(part, ref, buffer):
        for n in range(3):
            arrive(f"t{part}{n}", buffer.at[n])
        value = add(ref, buffer.at[0], buffer.at[1], buffer.at[2])
        mine = done.at[c, l, z, rest[part], lanes[part]]
        mine[...] = value
        send(f"gy{part}", mine, mine, twin)
        send(f"gp{part}", mine, mine, zp)
        send(f"gm{part}", mine, mine, zm)
        send(f"g2{part}", mine, mine, z2)

    def pass_on(part):
        def piece(ll, dz):
            return done.at[c, ll, wrap(z + dz), rest[part], lanes[part]]

        arrive(f"gy{part}", piece(1 - l, 0))
        send(f"fp{part}", piece(1 - l, 0), piece(1 - l, 0), zp)
        send(f"fm{part}", piece(1 - l, 0), piece(1 - l, 0), zm)
        arrive(f"g2{part}", piece(l, 2))
        send(f"fy{part}", piece(l, 2), piece(l, 2), twin)

    def collect(part):
        def piece(ll, dz):
            return done.at[c, ll, wrap(z + dz), rest[part], lanes[part]]

        arrive(f"gp{part}", piece(l, -1))
        arrive(f"gm{part}", piece(l, 1))
        arrive(f"fp{part}", piece(1 - l, -1))
        arrive(f"fm{part}", piece(1 - l, 1))
        arrive(f"fy{part}", piece(1 - l, 2))
        ref = done.at[c, :, :, rest[part], lanes[part]]
        send(f"e{part}", ref, ref, peer)

    finish(2, summed.at[h * 4 + x, piece_rows, lanes[2]], p2_three)
    finish(1, third1(0), p1_three)
    pass_on(2)
    finish(0, third0(0), p0_three)
    pass_on(1)
    collect(2)
    pass_on(0)
    collect(1)
    collect(0)
    for part in (2, 1, 0):
        arrive(f"e{part}", done.at[1 - c, :, :, rest[part], lanes[part]])
    out_copy = pltpu.make_async_copy(done, gt_out, local_sem.at[3])
    out_copy.start()
    for one in started:
        one.wait_send()
    for one in hg_copies:
        one.wait()
    out_copy.wait()


def main_call(counts, send_peer, recv_from, key_weight, value_weight, hidden, queries, out_grad):
    rows, width = key_weight.shape
    blocks, group = lax.axis_size("fsdp"), lax.axis_size("dp")
    slots, tokens, _ = hidden.shape
    total, cols, span, chips = slots * tokens, 2 * width, 2 * rows, blocks // 2
    bf16 = jnp.bfloat16
    smem = pl.BlockSpec(memory_space=pltpu.SMEM)
    vmem = pl.BlockSpec(memory_space=pltpu.VMEM)
    hbm = pl.BlockSpec(memory_space=pl.ANY)

    def buffer(*shape):
        return pltpu.VMEM(shape, bf16)

    return pl.pallas_call(
        main_kernel,
        name="main",
        out_shape=(
            jax.ShapeDtypeStruct(hidden.shape, bf16),
            jax.ShapeDtypeStruct((2, 2, 4, width // 8, span), bf16),
        ),
        in_specs=[smem, smem, smem, vmem, vmem, hbm, hbm, hbm],
        out_specs=(hbm, hbm),
        scratch_shapes=[
            buffer(blocks, rows, cols),
            buffer(*hidden.shape),
            buffer(*queries.shape),
            buffer(*out_grad.shape),
            pltpu.VMEM((total, cols), jnp.float32),
            buffer(total, cols),
            buffer(total, cols),
            buffer(group, tokens, cols),
            buffer(group, tokens, cols),
            buffer(total, cols),
            buffer(2, width, total),
            buffer(chips, width, span),
            buffer(chips, slots, tokens, span),
            buffer(chips, slots, tokens, span),
            buffer(2, width, 256),
            buffer(2, 2, width, 256),
            buffer(8, width // 8, 384),
            buffer(2, 8, width // 8, 384),
            buffer(4, width // 4, 384),
            buffer(2, 4, width // 4, 384),
            buffer(3, width // 2, 256),
            buffer(3, 2, width // 8, 384),
            buffer(3, 4, width // 16, 384),
            buffer(3, width // 8, 256),
            buffer(3, width // 16, 384),
            buffer(3, width // 16, 384),
            buffer(2, 2, 4, width // 8, span),
            pltpu.SemaphoreType.DMA((176,)),
            pltpu.SemaphoreType.DMA((176,)),
            pltpu.SemaphoreType.DMA((12,)),
        ],
        compiler_params=pltpu.CompilerParams(
            collective_id=0, has_side_effects=True, vmem_limit_bytes=62 << 20
        ),
        cost_estimate=pl.CostEstimate(
            flops=6 * total * blocks * rows * cols, bytes_accessed=22 << 20, transcendentals=0
        ),
    )(counts, send_peer, recv_from, key_weight, value_weight, hidden, queries, out_grad)


def finish_kernel(hg_in, pieces_in, hg_out, key_grad, value_grad, hg, pieces, sem):
    chunks = 8
    step = hg.shape[0] // chunks
    first = pltpu.make_async_copy(pieces_in, pieces, sem.at[2 * chunks])
    first.start()

    def chunk(i, src, dst, offset):
        at = pl.ds(i * step, step)
        return pltpu.make_async_copy(src.at[at], dst.at[at], sem.at[offset + i])

    for i in range(chunks):
        chunk(i, hg_in, hg, 0).start()
    first.wait()
    for i in range(chunks):
        chunk(i, hg_in, hg, 0).wait()
        chunk(i, hg, hg_out, chunks).start()
    core = lax.rem(lax.axis_index("fsdp"), 2)
    rows, width = key_grad.shape
    for t, out in enumerate((key_grad, value_grad)):
        left = pieces[t, :, :, :, :256].reshape(width, 256)
        upper = [pieces[t, l, z, :32, 256:] for z in range(4) for l in range(2)]
        lower = [pieces[t, l, z, 32:, 256:] for l in range(2) for z in range(4)]
        right = jnp.concatenate(upper + lower, axis=0)
        grads = jnp.concatenate([left, right], axis=1)
        grads = grads.astype(jnp.float32)
        out[...] = jnp.where(core == 0, grads[:, :rows], grads[:, rows:]).T
    for i in range(chunks):
        chunk(i, hg, hg_out, chunks).wait()


def finish(hidden_grad, pieces):
    rows, width = pieces.shape[-1] // 2, pieces.shape[1] * pieces.shape[2] * pieces.shape[3]
    vmem = pl.BlockSpec(memory_space=pltpu.VMEM)
    hbm = pl.BlockSpec(memory_space=pl.ANY)
    grad = jax.ShapeDtypeStruct((rows, width), jnp.float32)
    return pl.pallas_call(
        finish_kernel,
        name="finish",
        out_shape=(jax.ShapeDtypeStruct(hidden_grad.shape, hidden_grad.dtype), grad, grad),
        in_specs=[hbm, hbm],
        out_specs=(hbm, vmem, vmem),
        scratch_shapes=[
            pltpu.VMEM(hidden_grad.shape, hidden_grad.dtype),
            pltpu.VMEM(pieces.shape, pieces.dtype),
            pltpu.SemaphoreType.DMA((17,)),
        ],
        compiler_params=pltpu.CompilerParams(vmem_limit_bytes=60 << 20),
    )(hidden_grad, pieces)


def body(hidden, queries, out_grad, counts, send_peer, recv_from, key_weight, value_weight):
    hidden_grad, pieces = main_call(
        counts, send_peer, recv_from, key_weight, value_weight, hidden, queries, out_grad
    )
    return finish(hidden_grad, pieces)


def solution(mesh):
    return jax.shard_map(
        body,
        mesh=mesh,
        in_specs=(
            P(("dp", "fsdp"), None, None),
            P(("dp", "fsdp"), None, None),
            P(("dp", "fsdp"), None, None),
            P(("dp", "fsdp")),
            P(("dp", "fsdp")),
            P(("dp", "fsdp")),
            P("fsdp", None),
            P("fsdp", None),
        ),
        out_specs=(P(("dp", "fsdp"), None, None), P("fsdp", None), P("fsdp", None)),
        check_vma=False,
    )
```

time: 121 us -> 111 us (0.917)
  Pallas kernels: 116 us -> 110 us
  local copies, waits for them, and re-layouts: 3.05 us -> 0 us
    pallas_call x3 -> x1, Pallas kernels: 110 us -> 104 us  [main_call(): pl.pallas_call(main_kernel, name='main', out_shape=(jax.ShapeDtypeStruct(...]
    unnamed x12 -> x0, local copies, waits for them, and re-layouts: 1.96 us -> none
where the time goes in v1:
time: 111 us
  Pallas kernels  110 us (99%)
    pallas_call x1, Pallas kernels, main_call(): pl.pallas_call(main_kernel, name='main', out_shape=(jax.ShapeDtypeStruct(...  104 us
    pallas_call x1, Pallas kernels, finish(): pl.pallas_call(finish_kernel, name='finish', out_shape=(jax.ShapeDtypeStr...  6.04 us

profile of v1, /device:TPU:1, one launch (start us, length us, event | category | flops | bytes accessed | tf_op | source)
XLA Modules:
  0.0 110.6 jit_solution(2527347559252493587)
XLA Ops:
  0.6 103.7 %main.1 = (bf16[16,32,5120]{2,1,0:T(8,128)(2,1)}, bf16[2,2,4,64,640]{4,3,2,1,0:T(8,128)(2,1)}) custom-call(s32[16]{0:T(128)} %counts.1, s32[16]{0:T(128)} %send_peer.1, s32[16]{0:T(128)} %recv_from.1, bf16[320,512]{1,0:T(8,128)(2,1)} %kw.1, bf16[320,512]{1,0:T(8,128)(2,1)} %vw.1, bf16[16,32,5120]{2,1,0:T(8,128)(2,1)} %hidden.1, ...), custom_call_target="tpu_custom_call" | custom-call | flops 16106127360 | bytes 23068672 | tf_op jit(solution)/shard_map/main/pallas_call | solution.py:604
  104.4 6.0 %finish.1 = (bf16[16,32,5120]{2,1,0:T(8,128)(2,1)}, f32[320,512]{1,0:T(8,128)}, f32[320,512]{1,0:T(8,128)}) custom-call(bf16[16,32,5120]{2,1,0:T(8,128)(2,1)} %get-tuple-element.5.hg_in, bf16[2,2,4,64,640]{4,3,2,1,0:T(8,128)(2,1)} %get-tuple-element.6.pieces_in), custom_call_target="tpu_custom_call" | custom-call | tf_op jit(solution)/shard_map/finish/pallas_call | solution.py:689

commit v2 on v1

--- a/solution.py
+++ b/solution.py
@@ -7,7 +7,6 @@
 
 HD = 128
 JBLK = 16
-WIDE = 384
 MESH = pl.DeviceIdType.MESH
 
 
@@ -111,20 +110,24 @@
     peer = at(core=1 - c)
     twin, yo = device(x, h, 1 - l, z, c), device(x, 1 - h, 1 - l, z, c)
 
+    others = [(lax.rem(me + j, group), f) for j in range(1, group)]
+    others += [xp, xm, x2, yo, y2, peer]
+    barrier = pltpu.get_barrier_semaphore()
+    for other in others:
+        pl.semaphore_signal(barrier, inc=1, device_id=other, device_id_type=MESH)
+    own = (h * 4 + x) * 2 + c
+    shards = []
+    for i, shard in enumerate((kw, vw)):
+        dst = w.at[own, :, pl.ds(i * width, width)]
+        shards.append(pltpu.make_async_copy(shard, dst, local_sem.at[4 + i]))
+        shards[-1].start()
+    for one in shards:
+        one.wait()
     loads = []
     for i, (src, dst) in enumerate(((hidden, hid), (queries, qs), (out_grad, gs))):
         loads.append(pltpu.make_async_copy(src, dst, local_sem.at[i]))
         loads[-1].start()
     hid_copy = loads[0]
-    own = (h * 4 + x) * 2 + c
-    w[own, :, pl.ds(0, width)] = kw[...]
-    w[own, :, pl.ds(width, width)] = vw[...]
-
-    others = [(lax.rem(me + j, group), f) for j in range(1, group)]
-    others += [xp, xm, x2, yo, y2, peer]
-    barrier = pltpu.get_barrier_semaphore()
-    for other in others:
-        pl.semaphore_signal(barrier, inc=1, device_id=other, device_id_type=MESH)
     pl.semaphore_wait(barrier, len(others))
 
     number = {}
@@ -152,95 +155,56 @@
     def w_arrive(name, block, row, col):
         arrive(name, w.at[block, pl.ds(*row), pl.ds(*col)])
 
+    shared, paired, direct, wide = (512, 512), (256, 256), (0, 256), (0, 512)
+    shared_cut = ((512, 256), (768, 256))
+    paired_cut = ((256, 128), (384, 128))
+    whole, low, high = (0, rows), (0, rows // 2), (rows // 2, rows // 2)
+    my_rows = (pl.multiple_of(l * (rows // 2), rows // 2), rows // 2)
+    twin_rows = (pl.multiple_of((1 - l) * (rows // 2), rows // 2), rows // 2)
+    blocks_in = [(1, 0), (0, -1), (0, 1), (1, -1), (1, 1), (0, 2), (1, 2)]
+    side = (h, 1 - h)
+
     def block(hh, dx, core=c):
         return (hh * 4 + wrap(x + dx)) * 2 + core
 
+    def source(b, core=c):
+        return block(side[blocks_in[b][0]], blocks_in[b][1], core)
+
     def part(dz):
         return (pl.multiple_of(wrap(z + dz) * quarter, quarter), quarter)
 
-    def halves(odd):
-        first = 256 if odd else 384
-        return (WIDE, first), (WIDE + first, cols - WIDE - first)
-
-    side = (h, 1 - h)
-    narrow, wide = (WIDE, cols - WIDE), (0, WIDE)
-    whole, low, high = (0, rows), (0, rows // 2), (rows // 2, rows // 2)
-
-    w_send("cy", own, part(0), narrow, yo)
-    w_send("cxp0", own, part(0), narrow, xp)
-    w_send("cxm0", own, part(0), narrow, xm)
-    w_send("own", own, whole, (0, cols), peer)
-
-    def along_z(b, f):
-        w_send(f"zp{b}", f, part(0), narrow, zp)
-        w_send(f"zm{b}", f, part(0), narrow, zm)
-
-    blocks_in = [(1, 0), (0, -1), (0, 1), (1, -1), (1, 1), (0, 2), (1, 2)]
-
-    def source(b):
-        return block(side[blocks_in[b][0]], blocks_in[b][1])
-
-    w_arrive("cy", source(0), part(0), narrow)
-    w_send("cxp1", source(0), part(0), narrow, xp)
-    w_send("cxm1", source(0), part(0), narrow, xm)
-    along_z(0, source(0))
-    for s in (0, 1):
-        one, two = halves(s)
-        w_arrive(f"cxp{s}", block(side[s], -1), part(0), narrow)
-        w_send(f"cfp{s}", block(side[s], -1), part(0), one, xp)
-        w_arrive(f"cxm{s}", block(side[s], 1), part(0), narrow)
-        w_send(f"cfm{s}", block(side[s], 1), part(0), two, xm)
-        if s == 0:
-            along_z(1, source(1))
-            along_z(2, source(2))
-    w_send("ay", own, whole, wide, yo)
-    w_send("axp0", own, whole, wide, xp)
-    w_send("axm0", own, whole, wide, xm)
-    for s in (0, 1):
-        one, two = halves(s)
-        w_arrive(f"cfp{s}", source(5 + s), part(0), one)
-        w_arrive(f"cfm{s}", source(5 + s), part(0), two)
+    def along_z(b):
+        w_send(f"zp{b}", source(b), part(0), shared, zp)
+        w_send(f"zm{b}", source(b), part(0), shared, zm)
 
     def forward_z(b):
-        s, dx = blocks_in[b]
-        one, two = halves(b % 2)
-        f = block(side[s], dx)
-        w_arrive(f"zp{b}", f, part(-1), narrow)
-        w_send(f"zfp{b}", f, part(-1), one, zp)
-        w_arrive(f"zm{b}", f, part(1), narrow)
-        w_send(f"zfm{b}", f, part(1), two, zm)
+        w_arrive(f"zp{b}", source(b), part(-1), shared)
+        w_send(f"zfp{b}", source(b), part(-1), shared_cut[0], zp)
+        w_arrive(f"zm{b}", source(b), part(1), shared)
+        w_send(f"zfm{b}", source(b), part(1), shared_cut[1], zm)
 
     def finish_z(b):
-        s, dx = blocks_in[b]
-        one, two = halves(b % 2)
-        f = block(side[s], dx)
-        w_arrive(f"zfp{b}", f, part(2), one)
-        w_arrive(f"zfm{b}", f, part(2), two)
-        w_send(f"pc{b}", f, whole, narrow, peer)
-
-    def forward_x(s):
-        w_arrive(f"axp{s}", block(side[s], -1), whole, wide)
-        w_send(f"afp{s}", block(side[s], -1), low, wide, xp)
-        w_arrive(f"axm{s}", block(side[s], 1), whole, wide)
-        w_send(f"afm{s}", block(side[s], 1), high, wide, xm)
-        w_send(f"pa{1 + 2 * s}", block(side[s], -1), whole, wide, peer)
-        w_send(f"pa{2 + 2 * s}", block(side[s], 1), whole, wide, peer)
-
-    def finish_x(s):
-        w_arrive(f"afp{s}", source(5 + s), low, wide)
-        w_arrive(f"afm{s}", source(5 + s), high, wide)
-        w_send(f"pa{5 + s}", source(5 + s), whole, wide, peer)
+        w_arrive(f"zfp{b}", source(b), part(2), shared_cut[0])
+        w_arrive(f"zfm{b}", source(b), part(2), shared_cut[1])
+        w_send(f"pc{b}", source(b), whole, shared, peer)
+
+    def finish_wide(b):
+        w_arrive(f"td{b}", source(b), twin_rows, paired)
+        if b in (0, 3, 4, 6):
+            w_arrive(f"by{b}", source(b), whole, direct)
+        w_send(f"pa{b}", source(b), whole, wide, peer)
+
+    def to_twin(b):
+        w_send(f"td{b}", source(b), my_rows, paired, twin)
 
     def project(b):
         if b < 0:
             w_arrive("own", block(h, 0, 1 - c), whole, (0, cols))
             k = h * 4 + x
         else:
-            s, dx = blocks_in[b]
-            w_arrive(f"pa{b}", block(side[s], dx, 1 - c), whole, wide)
-            w_arrive(f"pc{b}", block(side[s], dx, 1 - c), whole, narrow)
-            k = side[s] * 4 + wrap(x + dx)
-        span = 2 * rows
+            w_arrive(f"pa{b}", source(b, 1 - c), whole, wide)
+            w_arrive(f"pc{b}", source(b, 1 - c), whole, shared)
+            k = side[blocks_in[b][0]] * 4 + wrap(x + blocks_in[b][1])
         left = pl.ds(pl.multiple_of(k * span, 128), span)
         right = pl.ds(pl.multiple_of(k * 2, 2), 2)
 
@@ -259,40 +223,87 @@
             else:
                 pair[:, at] = (acc[:, at] + value).astype(jnp.bfloat16)
 
+    w_send("cy", own, part(0), shared, yo)
+    w_send("cxp0", own, part(0), shared, xp)
+    w_send("cxm0", own, part(0), shared, xm)
+    w_send("dy", own, twin_rows, paired, yo)
+    w_send("bxp", own, whole, direct, xp)
+    w_send("bxm", own, whole, direct, xm)
+    w_send("by0", own, whole, direct, yo)
+    w_send("own", own, whole, (0, cols), peer)
+
+    w_arrive("cy", source(0), part(0), shared)
+    w_send("cxp1", source(0), part(0), shared, xp)
+    w_send("cxm1", source(0), part(0), shared, xm)
+    along_z(0)
+    w_arrive("cxp0", source(1), part(0), shared)
+    w_send("cfp0", source(1), part(0), shared_cut[0], xp)
+    along_z(1)
+    w_arrive("cxm0", source(2), part(0), shared)
+    w_send("cfm0", source(2), part(0), shared_cut[1], xm)
+    along_z(2)
+    w_send("dxp0", own, my_rows, paired, xp)
+    w_send("dxm0", own, my_rows, paired, xm)
+    w_arrive("dy", source(0), my_rows, paired)
+    to_twin(0)
+    w_arrive("cxp1", source(3), part(0), shared)
+    w_send("cfp1", source(3), part(0), shared_cut[0], xp)
+    w_arrive("cxm1", source(4), part(0), shared)
+    w_send("cfm1", source(4), part(0), shared_cut[1], xm)
+    w_send("dxp1", source(0), my_rows, paired, xp)
+    w_send("dxm1", source(0), my_rows, paired, xm)
     forward_z(0)
-    along_z(3, source(3))
+    along_z(3)
+    w_arrive("bxp", source(1), whole, direct)
+    w_send("by3", source(1), whole, direct, yo)
+    w_send("bfp", source(1), low, direct, xp)
+    w_arrive("bxm", source(2), whole, direct)
+    w_send("by4", source(2), whole, direct, yo)
+    w_send("bfm", source(2), high, direct, xm)
     forward_z(1)
-    along_z(4, source(4))
-    w_arrive("ay", source(0), whole, wide)
-    w_send("axp1", source(0), whole, wide, xp)
-    w_send("axm1", source(0), whole, wide, xm)
-    w_send("pa0", source(0), whole, wide, peer)
+    along_z(4)
     hid_copy.wait()
     project(-1)
+    for s in (0, 1):
+        w_arrive(f"cfp{s}", source(5 + s), part(0), shared_cut[0])
+        w_arrive(f"cfm{s}", source(5 + s), part(0), shared_cut[1])
     forward_z(2)
-    along_z(5, source(5))
+    along_z(5)
+    for s in (0, 1):
+        up, down = source(1 + 2 * s), source(2 + 2 * s)
+        w_arrive(f"dxp{s}", up, my_rows, paired)
+        w_send(f"dfp{s}", up, my_rows, paired_cut[0], xp)
+        to_twin(1 + 2 * s)
+        w_arrive(f"dxm{s}", down, my_rows, paired)
+        w_send(f"dfm{s}", down, my_rows, paired_cut[1], xm)
+        to_twin(2 + 2 * s)
     forward_z(3)
-    along_z(6, source(6))
-    forward_x(0)
+    along_z(6)
+    w_arrive("bfp", source(5), low, direct)
+    w_arrive("bfm", source(5), high, direct)
+    w_send("by6", source(5), whole, direct, yo)
+    for s in (0, 1):
+        w_arrive(f"dfp{s}", source(5 + s), my_rows, paired_cut[0])
+        w_arrive(f"dfm{s}", source(5 + s), my_rows, paired_cut[1])
+        to_twin(5 + s)
+    finish_wide(0)
     finish_z(0)
     forward_z(4)
+    finish_wide(1)
     finish_z(1)
     project(0)
     forward_z(5)
-    forward_x(1)
+    finish_wide(2)
     finish_z(2)
     project(1)
     forward_z(6)
+    finish_wide(3)
     finish_z(3)
     project(2)
-    finish_z(4)
-    project(3)
-    finish_x(0)
-    finish_z(5)
-    project(4)
-    finish_x(1)
-    finish_z(6)
-    project(5)
+    for b in (4, 5, 6):
+        finish_wide(b)
+        finish_z(b)
+        project(b - 1)
     project(6)
 
     loads[1].wait()
@@ -308,17 +319,19 @@
             value = value + ref[...].astype(f32)
         return value.astype(bf16)
 
-    arrived[me] = jnp.zeros(arrived.shape[1:], bf16)
-    for j in range(1, group):
-        to = lax.rem(me + j, group)
-        chosen = delta[pl.ds(0, tokens), :]
-        for s in range(1, slots):
-            here = delta[pl.ds(s * tokens, tokens), :]
-            chosen = jnp.where(send_peer[s] == to, here, chosen)
-        leaving[to] = chosen
-        send(f"a{j}", leaving.at[to], arrived.at[me], (to, f))
-    for t in (0, 1):
-        dt[t] = delta[:, t * half : (t + 1) * half].T
+    def leave():
+        arrived[me] = jnp.zeros(arrived.shape[1:], bf16)
+        for j in range(1, group):
+            to = lax.rem(me + j, group)
+            chosen = delta[pl.ds(0, tokens), :]
+            for s in range(1, slots):
+                here = delta[pl.ds(s * tokens, tokens), :]
+                chosen = jnp.where(send_peer[s] == to, here, chosen)
+            leaving[to] = chosen
+            send(f"a{j}", leaving.at[to], arrived.at[me], (to, f))
+
+    def turn(t):
+        dt[t] = delta[:, pl.ds(pl.multiple_of(t * half, half), half)].T
 
     lanes = (pl.ds(0, 256), pl.ds(256, 384), pl.ds(256, 384))
     rest = (pl.ds(0, 64), pl.ds(0, 32), pl.ds(32, 32))
@@ -401,8 +414,11 @@
     def xref(hh, dx):
         return summed.at[index(hh, dx), :, lanes[0]]
 
+    turn(1 - c)
     other_half(0)
+    leave()
     other_half(1)
+    turn(c)
     for i in range(8):
         own_half(i)
         if i == 0:
@@ -595,7 +611,6 @@
     total, cols, span, chips = slots * tokens, 2 * width, 2 * rows, blocks // 2
     bf16 = jnp.bfloat16
     smem = pl.BlockSpec(memory_space=pltpu.SMEM)
-    vmem = pl.BlockSpec(memory_space=pltpu.VMEM)
     hbm = pl.BlockSpec(memory_space=pl.ANY)
 
     def buffer(*shape):
@@ -608,7 +623,7 @@
             jax.ShapeDtypeStruct(hidden.shape, bf16),
             jax.ShapeDtypeStruct((2, 2, 4, width // 8, span), bf16),
         ),
-        in_specs=[smem, smem, smem, vmem, vmem, hbm, hbm, hbm],
+        in_specs=[smem, smem, smem, hbm, hbm, hbm, hbm, hbm],
         out_specs=(hbm, hbm),
         scratch_shapes=[
             buffer(blocks, rows, cols),
@@ -638,8 +653,8 @@
             buffer(3, width // 16, 384),
             buffer(3, width // 16, 384),
             buffer(2, 2, 4, width // 8, span),
-            pltpu.SemaphoreType.DMA((176,)),
-            pltpu.SemaphoreType.DMA((176,)),
+            pltpu.SemaphoreType.DMA((192,)),
+            pltpu.SemaphoreType.DMA((192,)),
             pltpu.SemaphoreType.DMA((12,)),
         ],
         compiler_params=pltpu.CompilerParams(

time: 111 us -> 108 us (0.973)
  Pallas kernels: 110 us -> 107 us
    pallas_call x1, Pallas kernels: 104 us -> 101 us  [main_call(): pl.pallas_call(main_kernel, name='main', out_shape=(jax.ShapeDtypeStruct(...]
where the time goes in v2:
time: 108 us; the launch traced here: 107 us
  Pallas kernels  107 us (99%)
    pallas_call x1, Pallas kernels, main_call(): pl.pallas_call(main_kernel, name='main', out_shape=(jax.ShapeDtypeStruct(...  101 us
    pallas_call x1, Pallas kernels, finish(): pl.pallas_call(finish_kernel, name='finish', out_shape=(jax.ShapeDtypeStr...  6.04 us

profile of v2, /device:TPU:1, one launch (start us, length us, event | category | flops | bytes accessed | tf_op | source)
XLA Modules:
  0.0 107.5 jit_solution(1152684748546395846)
XLA Ops:
  0.6 100.6 %main.1 = (bf16[16,32,5120]{2,1,0:T(8,128)(2,1)}, bf16[2,2,4,64,640]{4,3,2,1,0:T(8,128)(2,1)}) custom-call(s32[16]{0:T(128)} %counts.1, s32[16]{0:T(128)} %send_peer.1, s32[16]{0:T(128)} %recv_from.1, bf16[320,512]{1,0:T(8,128)(2,1)} %kw.1, bf16[320,512]{1,0:T(8,128)(2,1)} %vw.1, bf16[16,32,5120]{2,1,0:T(8,128)(2,1)} %hidden.1, ...), custom_call_target="tpu_custom_call" | custom-call | flops 16106127360 | bytes 23068672 | tf_op jit(solution)/shard_map/main/pallas_call | solution.py:619
  101.3 6.0 %finish.1 = (bf16[16,32,5120]{2,1,0:T(8,128)(2,1)}, f32[320,512]{1,0:T(8,128)}, f32[320,512]{1,0:T(8,128)}) custom-call(bf16[16,32,5120]{2,1,0:T(8,128)(2,1)} %get-tuple-element.5.hg_in, bf16[2,2,4,64,640]{4,3,2,1,0:T(8,128)(2,1)} %get-tuple-element.6.pieces_in), custom_call_target="tpu_custom_call" | custom-call | tf_op jit(solution)/shard_map/finish/pallas_call | solution.py:704

commit v3 on v2

--- a/solution.py
+++ b/solution.py
@@ -414,9 +414,9 @@
     def xref(hh, dx):
         return summed.at[index(hh, dx), :, lanes[0]]
 
+    leave()
     turn(1 - c)
     other_half(0)
-    leave()
     other_half(1)
     turn(c)
     for i in range(8):

time: 108 us -> 108 us (level)
  no operation moved by 1% of the time
where the time goes in v3:
time: 108 us
  Pallas kernels  107 us (99%)
    pallas_call x1, Pallas kernels, main_call(): pl.pallas_call(main_kernel, name='main', out_shape=(jax.ShapeDtypeStruct(...  101 us
    pallas_call x1, Pallas kernels, finish(): pl.pallas_call(finish_kernel, name='finish', out_shape=(jax.ShapeDtypeStr...  6.04 us

profile of v3, /device:TPU:1, one launch (start us, length us, event | category | flops | bytes accessed | tf_op | source)
XLA Modules:
  0.0 107.6 jit_solution(6316052687207091483)
XLA Ops:
  0.6 100.7 %main.1 = (bf16[16,32,5120]{2,1,0:T(8,128)(2,1)}, bf16[2,2,4,64,640]{4,3,2,1,0:T(8,128)(2,1)}) custom-call(s32[16]{0:T(128)} %counts.1, s32[16]{0:T(128)} %send_peer.1, s32[16]{0:T(128)} %recv_from.1, bf16[320,512]{1,0:T(8,128)(2,1)} %kw.1, bf16[320,512]{1,0:T(8,128)(2,1)} %vw.1, bf16[16,32,5120]{2,1,0:T(8,128)(2,1)} %hidden.1, ...), custom_call_target="tpu_custom_call" | custom-call | flops 16106127360 | bytes 23068672 | tf_op jit(solution)/shard_map/main/pallas_call | solution.py:619
  101.3 6.0 %finish.1 = (bf16[16,32,5120]{2,1,0:T(8,128)(2,1)}, f32[320,512]{1,0:T(8,128)}, f32[320,512]{1,0:T(8,128)}) custom-call(bf16[16,32,5120]{2,1,0:T(8,128)(2,1)} %get-tuple-element.5.hg_in, bf16[2,2,4,64,640]{4,3,2,1,0:T(8,128)(2,1)} %get-tuple-element.6.pieces_in), custom_call_target="tpu_custom_call" | custom-call | tf_op jit(solution)/shard_map/finish/pallas_call | solution.py:704
